TPU v7x, 32 devices: a whole 2x2x4 slice. The times are simulated.
32 devices in a mesh: row: 8 (over z, y), col: 4 (over x, core).
Axes of the slice: x: 2, y: 2, z: 4, core: 2. Of those that a mesh axis runs over, the one named last changes fastest.
Arguments:
- weights: float32 [192, 5, 256, 256], P(('row', 'col')), may hold values from 0.01 to 1
- band_mask: int32 [192, 5], P(('row', 'col')), may hold values from 0 to 1, as said below
- out_slots: int32 [192, 4], P(('row', 'col')), may hold values from -1 to 8, as said below
Outputs:
- flow: float32 [192, 4, 256, 256], P(('row', 'col'))
Inputs may be any that keep to these rules, and one draw needn't show every extreme that they name: `band_mask`: the diagonal block (t = 2) is always 1; blocks whose column lies outside the matrix are 0. `out_slots`: in each row the live entries come first, are distinct, name block columns inside the matrix, and the first is 4; the rest are -1. Row 0 has all 4 slots live.
All inputs are finite; a program needn't handle non-finite values.
Results may differ from a plain program's by a relative error of at most 0.0003.
Values sent between devices are 32-bit elements; how exact they have to be, the bound alone decides.
A program may use at most 128 MiB of HBM per device.

v0:
```python
import jax
import jax.numpy as jnp
from jax import lax
from jax.sharding import PartitionSpec as P

B = 256
W = 2
CAPO = 4
RBD = 6
NBAND = 5


highest = lax.Precision.HIGHEST


def passed_along(value, axis, by):
    devices = lax.axis_size(axis)
    pairs = [(i, i + by) for i in range(devices) if 0 <= i + by < devices]
    return lax.ppermute(value, axis, pairs)


def with_halo(cells, sides, width):
    for axis, dim in sides:
        count = lax.axis_size(axis)
        ends = count - 1
        head = lax.slice_in_dim(cells, 0, width, axis=dim)
        tail = lax.slice_in_dim(cells, cells.shape[dim] - width, cells.shape[dim], axis=dim)
        cells = jnp.concatenate(
            [
                lax.ppermute(tail, axis, [(i, (i + 1) % count) for i in range(ends)]),
                cells,
                lax.ppermute(head, axis, [((i + 1) % count, i) for i in range(ends)]),
            ],
            axis=dim,
        )
    return cells


def symmetrize(extended, row_count, inside, identity_band):
    own_rows = extended[W : W + row_count]
    mirrored = jnp.stack(
        [
            jnp.swapaxes(extended[offset : offset + row_count, 2 * W - offset], -1, -2)
            for offset in range(NBAND)
        ],
        axis=1,
    )
    return (
        0.5 * (own_rows + mirrored)
        + inside.astype(jnp.float32)[:, None, None, None] * identity_band
    )


def body(weights, band_mask, out_slots):
    masked_weights = weights * band_mask.astype(jnp.float32)[:, :, None, None]
    eye_block = jnp.eye(B, dtype=jnp.float32)
    identity_band = (jnp.arange(NBAND) == W).astype(jnp.float32)[:, None, None] * eye_block
    upper_part = passed_along(masked_weights[RBD - W :, W + 1 :], ("row", "col"), 1)
    lower_part = passed_along(masked_weights[:W, :W], ("row", "col"), -1)
    extended = jnp.zeros((RBD + 2 * W, NBAND, B, B), jnp.float32)
    extended = extended.at[W : W + RBD].set(masked_weights)
    extended = extended.at[:W, W + 1 :].set(upper_part)
    extended = extended.at[RBD + W :, :W].set(lower_part)
    symmetric_own = symmetrize(extended, RBD, jnp.ones((RBD,), jnp.bool_), identity_band)
    degree = jnp.sum(symmetric_own, axis=(1, 3))
    scaled = symmetric_own / degree[:, None, :, None]
    right_band = with_halo(scaled, ((("row", "col"), 0),), W)
    offsets = jnp.arange(NBAND, dtype=jnp.int32)

    def expand_local(local_row):
        slot_ids = out_slots[local_row]
        live_slot = slot_ids >= 0
        band_pick = slot_ids[:, None] - offsets[None, :]
        usable = live_slot[:, None] & (band_pick >= 0) & (band_pick <= 2 * W)
        picked = jnp.clip(band_pick, 0, 2 * W)
        source_rows = local_row + offsets
        right_rows = (
            right_band[source_rows[None, :], picked] * usable.astype(jnp.float32)[:, :, None, None]
        )
        left_rows = symmetric_own[local_row]
        expanded = jnp.einsum("tij,stjk->sik", left_rows, right_rows, precision=highest)
        return expanded * expanded

    inflated = lax.map(expand_local, jnp.arange(RBD, dtype=jnp.int32))
    live_all = out_slots >= 0
    block_sums = jnp.sum(inflated, axis=2).reshape(RBD * CAPO, B)
    positions = jnp.arange(RBD, dtype=jnp.int32)[:, None] + out_slots
    columns = jnp.arange(RBD + 4 * W, dtype=jnp.int32)
    onehot = (
        ((positions[:, :, None] == columns) & live_all[:, :, None])
        .astype(jnp.float32)
        .reshape(RBD * CAPO, RBD + 4 * W)
    )
    partial_value = jnp.dot(
        onehot.T, block_sums, precision=highest, preferred_element_type=jnp.float32
    )
    neighbour_parts = with_halo(partial_value, ((("row", "col"), 0),), 2 * W)
    left_add = jnp.pad(neighbour_parts[: 2 * W], ((0, RBD - 2 * W), (0, 0)))
    right_add = jnp.pad(neighbour_parts[-2 * W :], ((RBD - 2 * W, 0), (0, 0)))
    own_totals = partial_value[2 * W : 2 * W + RBD] + left_add + right_add
    near_totals = with_halo(own_totals, ((("row", "col"), 0),), 2 * W)
    slot_totals = jnp.dot(
        onehot, near_totals, precision=highest, preferred_element_type=jnp.float32
    ).reshape(RBD, CAPO, B)
    safe_total = jnp.where(live_all[:, :, None], slot_totals, jnp.float32(1.0))
    return jnp.where(
        live_all[:, :, None, None], B * inflated / safe_total[:, :, None, :], jnp.float32(0.0)
    )


def solution(mesh):
    return jax.shard_map(
        body,
        mesh=mesh,
        in_specs=(
            P(("row", "col"), None, None, None),
            P(("row", "col"), None),
            P(("row", "col"), None),
        ),
        out_specs=P(("row", "col"), None, None, None),
        check_vma=False,
    )
```

profile of v0, /device:TPU:0, one launch (start us, length us, event | category | flops | bytes accessed | tf_op | source)
XLA Modules:
  0.0 354.6 jit_solution(7885819918680084991)
XLA Ops:
  0.0 9.1 %copy.20 = f32[6,5,256,256]{2,3,0,1:T(8,128)} copy(f32[6,5,256,256]{3,2,1,0:T(8,128)} %param.11) | data formatting | bytes 15728640 | tf_op args[0]
  9.2 4.1 %broadcast_multiply_fusion = f32[6,5,256,256]{2,3,0,1:T(8,128)S(1)} fusion(f32[6,5,256,256]{2,3,0,1:T(8,128)} %copy.20, f32[6,5]{0,1:T(8,128)S(1)} %copy.19), kind=kLoop, calls=%fused_computation.35 | loop fusion | flops 1966080 | bytes 15728760 | tf_op jit(solution)/shard_map/mul | solution.py:55
  16.9 6.2 %scatter.10 = f32[10,5,256,256]{2,3,0,1:T(8,128)} pad(f32[6,5,256,256]{2,3,0,1:T(8,128)S(1)} %broadcast_multiply_fusion, f32[]{:T(128)} %constant.111.clone.1), padding=2_2x0_0x0_0x0_0 | pad | bytes 20971524 | tf_op jit(solution)/shard_map/scatter | solution.py:61
  29.0 9.5 %collective-permute-done.1 = f32[2,2,256,256]{2,3,0,1:T(8,128)S(1)} collective-permute-done((f32[2,2,256,256]{2,3,0,1:T(8,128)S(1)}, f32[2,2,256,256]{2,3,0,1:T(8,128)S(1)}, u32[]{:S(2)}, u32[]{:S(2)}) %collective-permute-start.1) | collective-permute-done | bytes 1048608 | tf_op jit(solution)/shard_map/ppermute | solution.py:19
  42.4 7.2 %slice.161 = f32[6,5,256,256]{2,3,0,1:T(8,128)} slice(f32[10,5,256,256]{2,3,0,1:T(8,128)} %constant_dynamic-update-slice_fusion), slice={[2:8], [0:5], [0:256], [0:256]} | slice | bytes 15728640 | tf_op jit(solution)/shard_map/slice | solution.py:40
  60.6 9.1 %copy.25 = f32[6,5,256,256]{3,2,1,0:T(8,128)} copy(f32[6,5,256,256]{2,3,0,1:T(8,128)} %slice.161) | data formatting | bytes 15728640 | tf_op jit(solution)/shard_map/slice | solution.py:40
  69.6 9.7 %fusion.55 = (f32[6,256]{1,0:T(8,128)S(1)}, f32[6,5,256,256]{3,2,1,0:T(8,128)}) fusion(f32[5,256,256]{2,1,0:T(8,128)S(1)} %broadcast_multiply_fusion.1, f32[6,5,256,256]{3,2,1,0:T(8,128)} %copy.25, f32[6,5,256,256]{3,2,1,0:T(8,128)} %fusion.32), kind=kLoop, calls=%fused_computation.75 | loop fusion | flops 7862784 | bytes 24909824 | tf_op jit(solution)/shard_map/reduce_sum | solution.py:65
  79.3 4.2 %broadcast_divide_fusion = f32[6,5,256,256]{3,2,1,0:T(8,128)S(1)} fusion(f32[6,5,256,256]{3,2,1,0:T(8,128)} %get-tuple-element.202, f32[6,256]{1,0:T(8,128)S(1)} %get-tuple-element.144), kind=kLoop, calls=%fused_computation.34 | loop fusion | flops 1966080 | bytes 15734784 | tf_op jit(solution)/shard_map/div | solution.py:66
  89.3 14.8 %collective-permute-start.2 = (f32[2,5,256,256]{3,2,1,0:T(8,128)}, f32[2,5,256,256]{3,2,1,0:T(8,128)S(1)}, u32[]{:S(2)}, u32[]{:S(2)}) collective-permute-start(f32[2,5,256,256]{3,2,1,0:T(8,128)} %get-tuple-element.146), channel_id=1, source_target_pairs={{0,1},{1,2},{2,3},{3,4},{4,5},{5,6},{6,7},{7,8},{8,9},{9,10},{10,1... | collective-permute-start | bytes 7864328 | tf_op jit(solution)/shard_map/ppermute | solution.py:30
  111.2 9.0 %pad_maximum_fusion = f32[10,5,256,256]{3,2,1,0:T(8,128)} fusion(f32[2,5,256,256]{3,2,1,0:T(8,128)} %collective-permute-done.3, f32[6,5,256,256]{3,2,1,0:T(8,128)} %copy-done, f32[2,5,256,256]{3,2,1,0:T(8,128)S(1)} %collective-permute-done.2), kind=kLoop, calls=%fused_computation.31 | loop fusion | flops 6553600 | bytes 26214400 | tf_op jit(solution)/shard_map/concatenate | solution.py:28
  120.2 154.6 %while.15 = (s32[]{:T(128)}, f32[6,4,256,256]{2,3,1,0:T(8,128)}, s32[6]{0:T(128)S(1)}, s32[6,4]{1,0:T(8,128)S(1)}, f32[10,5,256,256]{3,2,1,0:T(8,128)}, /*index=...) while((s32[]{:T(128)}, f32[6,4,256,256]{2,3,1,0:T(8,128)}, ...), condition=%wide.region_3.0_spmd.clone.clone, body=%wide.region_2.0_spmd.clone.clone.sunk | while | flops 4028104960 | bytes 28575032 | solution.py:84
  123.8 8.1 %gather_fusion = f32[20,256,256]{2,1,0:T(8,128)} fusion(f32[10,5,256,256]{3,2,1,0:T(8,128)} %get-tuple-element.219, s32[20]{0:T(128)S(1)} %reshape.299), kind=kCustom, calls=%fused_computation.clone.clone.1 | custom fusion | bytes 10485920 | tf_op jit(solution)/shard_map/while/body/eval_jaxpr/gather | solution.py:78
  132.0 5.9 %copy.40 = f32[4,5,256,256]{2,3,1,0:T(8,128)} copy(f32[4,5,256,256]{3,2,1,0:T(8,128)} %bitcast.91) | data formatting | bytes 10485760 | tf_op jit(solution)/shard_map/while/body/eval_jaxpr/gather | solution.py:78
  137.9 8.1 %fusion.72 = f32[6,4,256,256]{2,3,1,0:T(8,128)} fusion(f32[6,4,256,256]{2,3,1,0:T(8,128)} %get-tuple-element.207, s32[]{:T(128)} %get-tuple-element.206, f32[4,5,256,256]{2,3,1,0:T(8,128)} %copy.40, f32[4,5]{1,0:T(4,128)S(1)} %fusion.71, f32[6,5,256,256]{3,2,1,0:T(8,128)} %get-tuple-element.220, s32[]{:T(128)S(6)} %select_n.56), kind=kOutput, calls=%fused_computation.8.clone.1 | convolution fusion | flops 4028104704 | bytes 7602772 | tf_op jit(solution)/shard_map/while/body/eval_jaxpr/tij,stjk->sik/dot_general | solution.py:81
  149.6 8.1 %gather_fusion = f32[20,256,256]{2,1,0:T(8,128)} fusion(f32[10,5,256,256]{3,2,1,0:T(8,128)} %get-tuple-element.219, s32[20]{0:T(128)S(1)} %reshape.299), kind=kCustom, calls=%fused_computation.clone.clone.1 | custom fusion | bytes 10485920 | tf_op jit(solution)/shard_map/while/body/eval_jaxpr/gather | solution.py:78
  157.7 5.9 %copy.40 = f32[4,5,256,256]{2,3,1,0:T(8,128)} copy(f32[4,5,256,256]{3,2,1,0:T(8,128)} %bitcast.91) | data formatting | bytes 10485760 | tf_op jit(solution)/shard_map/while/body/eval_jaxpr/gather | solution.py:78
  163.7 8.1 %fusion.72 = f32[6,4,256,256]{2,3,1,0:T(8,128)} fusion(f32[6,4,256,256]{2,3,1,0:T(8,128)} %get-tuple-element.207, s32[]{:T(128)} %get-tuple-element.206, f32[4,5,256,256]{2,3,1,0:T(8,128)} %copy.40, f32[4,5]{1,0:T(4,128)S(1)} %fusion.71, f32[6,5,256,256]{3,2,1,0:T(8,128)} %get-tuple-element.220, s32[]{:T(128)S(6)} %select_n.56), kind=kOutput, calls=%fused_computation.8.clone.1 | convolution fusion | flops 4028104704 | bytes 7602772 | tf_op jit(solution)/shard_map/while/body/eval_jaxpr/tij,stjk->sik/dot_general | solution.py:81
  175.4 8.1 %gather_fusion = f32[20,256,256]{2,1,0:T(8,128)} fusion(f32[10,5,256,256]{3,2,1,0:T(8,128)} %get-tuple-element.219, s32[20]{0:T(128)S(1)} %reshape.299), kind=kCustom, calls=%fused_computation.clone.clone.1 | custom fusion | bytes 10485920 | tf_op jit(solution)/shard_map/while/body/eval_jaxpr/gather | solution.py:78
  183.5 5.9 %copy.40 = f32[4,5,256,256]{2,3,1,0:T(8,128)} copy(f32[4,5,256,256]{3,2,1,0:T(8,128)} %bitcast.91) | data formatting | bytes 10485760 | tf_op jit(solution)/shard_map/while/body/eval_jaxpr/gather | solution.py:78
  189.4 8.1 %fusion.72 = f32[6,4,256,256]{2,3,1,0:T(8,128)} fusion(f32[6,4,256,256]{2,3,1,0:T(8,128)} %get-tuple-element.207, s32[]{:T(128)} %get-tuple-element.206, f32[4,5,256,256]{2,3,1,0:T(8,128)} %copy.40, f32[4,5]{1,0:T(4,128)S(1)} %fusion.71, f32[6,5,256,256]{3,2,1,0:T(8,128)} %get-tuple-element.220, s32[]{:T(128)S(6)} %select_n.56), kind=kOutput, calls=%fused_computation.8.clone.1 | convolution fusion | flops 4028104704 | bytes 7602772 | tf_op jit(solution)/shard_map/while/body/eval_jaxpr/tij,stjk->sik/dot_general | solution.py:81
  201.1 8.1 %gather_fusion = f32[20,256,256]{2,1,0:T(8,128)} fusion(f32[10,5,256,256]{3,2,1,0:T(8,128)} %get-tuple-element.219, s32[20]{0:T(128)S(1)} %reshape.299), kind=kCustom, calls=%fused_computation.clone.clone.1 | custom fusion | bytes 10485920 | tf_op jit(solution)/shard_map/while/body/eval_jaxpr/gather | solution.py:78
  209.3 5.9 %copy.40 = f32[4,5,256,256]{2,3,1,0:T(8,128)} copy(f32[4,5,256,256]{3,2,1,0:T(8,128)} %bitcast.91) | data formatting | bytes 10485760 | tf_op jit(solution)/shard_map/while/body/eval_jaxpr/gather | solution.py:78
  215.2 8.1 %fusion.72 = f32[6,4,256,256]{2,3,1,0:T(8,128)} fusion(f32[6,4,256,256]{2,3,1,0:T(8,128)} %get-tuple-element.207, s32[]{:T(128)} %get-tuple-element.206, f32[4,5,256,256]{2,3,1,0:T(8,128)} %copy.40, f32[4,5]{1,0:T(4,128)S(1)} %fusion.71, f32[6,5,256,256]{3,2,1,0:T(8,128)} %get-tuple-element.220, s32[]{:T(128)S(6)} %select_n.56), kind=kOutput, calls=%fused_computation.8.clone.1 | convolution fusion | flops 4028104704 | bytes 7602772 | tf_op jit(solution)/shard_map/while/body/eval_jaxpr/tij,stjk->sik/dot_general | solution.py:81
  226.9 8.1 %gather_fusion = f32[20,256,256]{2,1,0:T(8,128)} fusion(f32[10,5,256,256]{3,2,1,0:T(8,128)} %get-tuple-element.219, s32[20]{0:T(128)S(1)} %reshape.299), kind=kCustom, calls=%fused_computation.clone.clone.1 | custom fusion | bytes 10485920 | tf_op jit(solution)/shard_map/while/body/eval_jaxpr/gather | solution.py:78
  235.1 5.9 %copy.40 = f32[4,5,256,256]{2,3,1,0:T(8,128)} copy(f32[4,5,256,256]{3,2,1,0:T(8,128)} %bitcast.91) | data formatting | bytes 10485760 | tf_op jit(solution)/shard_map/while/body/eval_jaxpr/gather | solution.py:78
  241.0 8.1 %fusion.72 = f32[6,4,256,256]{2,3,1,0:T(8,128)} fusion(f32[6,4,256,256]{2,3,1,0:T(8,128)} %get-tuple-element.207, s32[]{:T(128)} %get-tuple-element.206, f32[4,5,256,256]{2,3,1,0:T(8,128)} %copy.40, f32[4,5]{1,0:T(4,128)S(1)} %fusion.71, f32[6,5,256,256]{3,2,1,0:T(8,128)} %get-tuple-element.220, s32[]{:T(128)S(6)} %select_n.56), kind=kOutput, calls=%fused_computation.8.clone.1 | convolution fusion | flops 4028104704 | bytes 7602772 | tf_op jit(solution)/shard_map/while/body/eval_jaxpr/tij,stjk->sik/dot_general | solution.py:81
  252.7 8.1 %gather_fusion = f32[20,256,256]{2,1,0:T(8,128)} fusion(f32[10,5,256,256]{3,2,1,0:T(8,128)} %get-tuple-element.219, s32[20]{0:T(128)S(1)} %reshape.299), kind=kCustom, calls=%fused_computation.clone.clone.1 | custom fusion | bytes 10485920 | tf_op jit(solution)/shard_map/while/body/eval_jaxpr/gather | solution.py:78
  260.8 5.9 %copy.40 = f32[4,5,256,256]{2,3,1,0:T(8,128)} copy(f32[4,5,256,256]{3,2,1,0:T(8,128)} %bitcast.91) | data formatting | bytes 10485760 | tf_op jit(solution)/shard_map/while/body/eval_jaxpr/gather | solution.py:78
  266.7 8.1 %fusion.72 = f32[6,4,256,256]{2,3,1,0:T(8,128)} fusion(f32[6,4,256,256]{2,3,1,0:T(8,128)} %get-tuple-element.207, s32[]{:T(128)} %get-tuple-element.206, f32[4,5,256,256]{2,3,1,0:T(8,128)} %copy.40, f32[4,5]{1,0:T(4,128)S(1)} %fusion.71, f32[6,5,256,256]{3,2,1,0:T(8,128)} %get-tuple-element.220, s32[]{:T(128)S(6)} %select_n.56), kind=kOutput, calls=%fused_computation.8.clone.1 | convolution fusion | flops 4028104704 | bytes 7602772 | tf_op jit(solution)/shard_map/while/body/eval_jaxpr/tij,stjk->sik/dot_general | solution.py:81
  278.8 54.1 %collective-permute-start.4 = (f32[4,256]{1,0:T(4,128)S(1)}, f32[4,256]{1,0:T(4,128)S(1)}, u32[]{:S(2)}, u32[]{:S(2)}) collective-permute-start(f32[4,256]{1,0:T(4,128)S(1)} %get-tuple-element.150), channel_id=1, source_target_pairs={{0,1},{1,2},{2,3},{3,4},{4,5},{5,6},{6,7},{7,8},{8,9},{9,10},{10,1... | collective-permute-start | bytes 12296 | tf_op jit(solution)/shard_map/ppermute | solution.py:30
  341.2 6.6 %copy.28 = f32[6,4,256,256]{3,2,1,0:T(8,128)} copy(f32[6,4,256,256]{2,3,1,0:T(8,128)} %get-tuple-element.84) | data formatting | bytes 12582912 | tf_op jit(solution)/shard_map/while | solution.py:84
  348.1 6.5 %divide_select_fusion = f32[6,4,256,256]{3,2,1,0:T(8,128)} fusion(f32[6,4,256,256]{3,2,1,0:T(8,128)} %copy.28, f32[6,4,256]{2,1,0:T(4,128)S(1)} %copy.30, pred[6,4]{1,0:T(8,128)(4,1)S(1)} %copy.18), kind=kLoop, calls=%fused_computation.33 | loop fusion | flops 4718592 | bytes 12607512 | tf_op jit(solution)/shard_map/jit(_where)/select_n | solution.py:106
  (87 shorter events, 59.2 us)
Async XLA Ops:
  0.0 9.1 %copy-start.2 = (s32[6,5]{1,0:T(8,128)S(1)}, s32[6,5]{1,0:T(8,128)}, u32[]{:S(2)}) copy-start(s32[6,5]{1,0:T(8,128)} %param.12) | copy-start | bytes 364
  14.3 9.3 %copy-start.3 = (s32[4]{0:T(128)S(1)}, s32[4]{0:T(128)}, u32[]{:S(2)}) copy-start(s32[4]{0:T(128)} %constant.114.clone.1) | copy-start | bytes 52
  14.3 10.1 %collective-permute-start = (f32[2,2,256,256]{2,3,0,1:T(8,128)}, f32[2,2,256,256]{2,3,0,1:T(8,128)S(1)}, u32[]{:S(2)}, u32[]{:S(2)}) collective-permute-start(f32[2,2,256,256]{2,3,0,1:T(8,128)} %slice.159), channel_id=1, source_target_pairs={{0,1},{1,2},{2,3},{3,4},{4,5},{5,6},{6,7},{7,8},{8,9},{9,10},{10,1... | collective-permute-start | bytes 3145736 | tf_op jit(solution)/shard_map/ppermute | solution.py:19
  27.5 11.1 %collective-permute-start.1 = (f32[2,2,256,256]{2,3,0,1:T(8,128)S(1)}, f32[2,2,256,256]{2,3,0,1:T(8,128)S(1)}, u32[]{:S(2)}, u32[]{:S(2)}) collective-permute-start(f32[2,2,256,256]{2,3,0,1:T(8,128)S(1)} %get-tuple-element.148), channel_id=1, source_target_pairs={{1,0},{2,1},{3,2},{4,3},{5,4},{6,5},{7,6},{8,7},{9,8},{10,9},{11,1... | collective-permute-start | bytes 3145736 | tf_op jit(solution)/shard_map/ppermute | solution.py:19
  83.5 3.1 copy-start
  86.6 19.0 %copy-start.1 = (s32[6,4]{0,1:T(4,128)S(1)}, s32[6,4]{0,1:T(4,128)}, u32[]{:S(2)}) copy-start(s32[6,4]{0,1:T(4,128)} %param.13) | copy-start | bytes 292
  89.3 19.3 %collective-permute-start.2 = (f32[2,5,256,256]{3,2,1,0:T(8,128)}, f32[2,5,256,256]{3,2,1,0:T(8,128)S(1)}, u32[]{:S(2)}, u32[]{:S(2)}) collective-permute-start(f32[2,5,256,256]{3,2,1,0:T(8,128)} %get-tuple-element.146), channel_id=1, source_target_pairs={{0,1},{1,2},{2,3},{3,4},{4,5},{5,6},{6,7},{7,8},{8,9},{9,10},{10,1... | collective-permute-start | bytes 7864328 | tf_op jit(solution)/shard_map/ppermute | solution.py:30
  104.0 7.1 %collective-permute-start.3 = (f32[2,5,256,256]{3,2,1,0:T(8,128)}, f32[2,5,256,256]{3,2,1,0:T(8,128)}, u32[]{:S(2)}, u32[]{:S(2)}) collective-permute-start(f32[2,5,256,256]{3,2,1,0:T(8,128)} %get-tuple-element.147), channel_id=1, source_target_pairs={{1,0},{2,1},{3,2},{4,3},{5,4},{6,5},{7,6},{8,7},{9,8},{10,9},{11,1... | collective-permute-start | bytes 7864328 | tf_op jit(solution)/shard_map/ppermute | solution.py:32
  278.8 55.4 %collective-permute-start.4 = (f32[4,256]{1,0:T(4,128)S(1)}, f32[4,256]{1,0:T(4,128)S(1)}, u32[]{:S(2)}, u32[]{:S(2)}) collective-permute-start(f32[4,256]{1,0:T(4,128)S(1)} %get-tuple-element.150), channel_id=1, source_target_pairs={{0,1},{1,2},{2,3},{3,4},{4,5},{5,6},{6,7},{7,8},{8,9},{9,10},{10,1... | collective-permute-start | bytes 12296 | tf_op jit(solution)/shard_map/ppermute | solution.py:30
  332.9 3.1 collective-permute-start.5
  336.0 11.8 %collective-permute-start.6 = (f32[4,256]{1,0:T(4,128)S(1)}, f32[4,256]{1,0:T(4,128)S(1)}, u32[]{:S(2)}, u32[]{:S(2)}) collective-permute-start(f32[4,256]{1,0:T(4,128)S(1)} %get-tuple-element.152), channel_id=1, source_target_pairs={{0,1},{1,2},{2,3},{3,4},{4,5},{5,6},{6,7},{7,8},{8,9},{9,10},{10,1... | collective-permute-start | bytes 12296 | tf_op jit(solution)/shard_map/ppermute | solution.py:30
  339.8 8.0 %collective-permute-start.7 = (f32[4,256]{1,0:T(4,128)S(1)}, f32[4,256]{1,0:T(4,128)S(1)}, u32[]{:S(2)}, u32[]{:S(2)}) collective-permute-start(f32[4,256]{1,0:T(4,128)S(1)} %get-tuple-element.153), channel_id=1, source_target_pairs={{1,0},{2,1},{3,2},{4,3},{5,4},{6,5},{7,6},{8,7},{9,8},{10,9},{11,1... | collective-permute-start | bytes 12296 | tf_op jit(solution)/shard_map/ppermute | solution.py:32
where the time goes:
time: 358 us; the launch traced here: 355 us
  local copies, waits for them, and re-layouts  149 us (42%)
  starting transfers between devices  80.6 us (23%)
  matrix products  49.2 us (14%)
  other arithmetic  46.3 us (13%)
  waiting for transfers between devices  16.8 us (5%)
  loops' own time  12.2 us (3%)
    gather x12, local copies, waits for them, and re-layouts, expand_local(): right_band[source_rows[None, :], picked]  84.3 us
    ppermute x3, starting transfers between devices, with_halo(): lax.ppermute(tail, axis, [(i, (i + 1) % count) for i in range(ends)])  72.7 us
    dot_general x6, matrix products, expand_local(): jnp.einsum('tij,stjk->sik', left_rows, right_rows, precision=highest)  48.7 us
    unnamed x14, local copies, waits for them, and re-layouts  23.3 us
    slice x2, local copies, waits for them, and re-layouts, symmetrize(): own_rows = extended[W:W + row_count]  16.2 us
    another operation x1, loops' own time, body(): inflated = lax.map(expand_local, jnp.arange(RBD, dtype=jnp.int32))  12.2 us
    reduce_sum x1, other arithmetic, body(): degree = jnp.sum(symmetric_own, axis=(1, 3))  9.67 us
    ppermute x2, waiting for transfers between devices, passed_along(): return lax.ppermute(value, axis, pairs)  9.55 us
  transfers between devices with their start and end apart: 8, of which 4 were waited for; matrix products, arithmetic and copies ran while one was open for 4% of the time, Pallas kernels for 0%

commit v1 on v0

v1 whole, which is shorter than its diff:
```python
import functools

import jax
import jax.numpy as jnp
from jax import lax
from jax.experimental import pallas as pl
from jax.experimental.pallas import tpu as pltpu
from jax.sharding import PartitionSpec as P

B = 256
NBAND = 5
CAPO = 4
ROWS = 6
SLOTS = ROWS * CAPO
BLOCKS = ROWS * NBAND
COLS = 16
F32, BF16 = jnp.float32, jnp.bfloat16
MESH = pl.DeviceIdType.MESH
CROSS = ((1, 0, 5), (28, 29, 24))
LANDS = (0, 2, 1)
INNER = ((3, 4, 8, 9), (26, 25, 21, 20))
DIAG = ((2, 7), (27, 22))
HIGHEST = lax.Precision.HIGHEST


def split(x):
    high = x.astype(BF16)
    return high, (x - high.astype(F32)).astype(BF16)


def dot(a, b):
    return jnp.dot(a, b, preferred_element_type=F32)


def dot_nt(a, b):
    return lax.dot_general(a, b, (((1,), (1,)), ((), ())), preferred_element_type=F32)


def product(a, b, mul=dot):
    return mul(a[0], b[0]) + (mul(a[0], b[1]) + mul(a[1], b[0]))


def kernel(
    names, sizes,
    slots, w_hbm, maskf, pick, put,
    inflated, scale,
    w, right_h, right_l, left_h, left_l, extra, packed, w_in, m_in, m_h, m_l, lx_h, lx_l,
    dinv, d_out, d_in, sums, part, part_in, totals,
    load_sem, w_send, w_recv, m_send, m_recv, d_send, d_recv, p_send, p_recv,
):
    ncol = sizes[1]
    count = sizes[0] * sizes[1]
    me = lax.axis_index(names[0]) * ncol + lax.axis_index(names[1])

    def at(by):
        there = me + by
        return (lax.div(there, ncol), lax.rem(there, ncol))

    def exists(by):
        return (me + by >= 0) & (me + by < count)

    steps = (-1, 1)
    far = (-1, 1, -2, 2)

    loads = [
        pltpu.make_async_copy(w_hbm.at[pl.ds(lo, n)], w.at[pl.ds(lo, n)], load_sem.at[j])
        for j, (lo, n) in enumerate(((0, 2), (5, 1), (24, 1), (28, 2), (2, 3), (6, 18), (25, 3)))
    ]
    for copy in loads:
        copy.start()

    barrier = pltpu.get_barrier_semaphore()
    for by in far:

        @pl.when(exists(by))
        def _():
            pl.semaphore_signal(barrier, inc=1, device_id=at(by), device_id_type=MESH)

    for copy in loads[:4]:
        copy.wait()
    for j in (0, 1, 5, 24, 28, 29):
        w[j] = w[j] * maskf[j]

    peers = sum(exists(by).astype(jnp.int32) for by in far)
    pl.semaphore_wait(barrier, peers)

    def remote(src, dst, ssem, rsem, by):
        return pltpu.make_async_remote_copy(
            src_ref=src, dst_ref=dst, send_sem=ssem, recv_sem=rsem, device_id=at(by), device_id_type=MESH
        )

    def w_copy(side, a, land_side, land):
        return remote(
            w.at[CROSS[side][a]], w_in.at[land_side, land],
            w_send.at[side, a], w_recv.at[land_side, land], steps[side],
        )

    def m_copy(side, a, land_side):
        src = packed.at[side] if a == 0 else w.at[INNER[side][a - 1]]
        return remote(src, m_in.at[land_side, a], m_send.at[side, a], m_recv.at[land_side, a], steps[side])

    def d_copy(side, land_side):
        return remote(d_out.at[side], d_in.at[land_side], d_send.at[side], d_recv.at[land_side], steps[side])

    def p_copy(j, land):
        return remote(part, part_in.at[land], p_send.at[j], p_recv.at[land], far[j])

    for side in range(2):

        @pl.when(exists(steps[side]))
        def _():
            for a in range(3):
                w_copy(side, a, 1 - side, LANDS[a]).start()

    zero = jnp.zeros((B, B), F32)
    for side in range(2):

        @pl.when(jnp.logical_not(exists(steps[side])))
        def _():
            for a in range(3):
                w_in[side, a] = zero
            for a in range(5):
                m_in[side, a] = zero
            d_in[side] = jnp.ones((8, B), F32)

    for j in range(4):

        @pl.when(jnp.logical_not(exists(far[j])))
        def _():
            part_in[j] = jnp.zeros((COLS, B), F32)

    for copy in loads[4:]:
        copy.wait()

    rows = lax.broadcasted_iota(jnp.int32, (B, B), 0)
    cols = lax.broadcasted_iota(jnp.int32, (B, B), 1)
    eye = (rows == cols).astype(F32)

    def diagonal(n, carry):
        j = n * NBAND + 2
        x = w[j] * maskf[j]
        s = 0.5 * (x + x.T) + eye
        w[j] = s
        h, l = split(s)
        right_h[j], right_l[j] = h, l
        return carry

    lax.fori_loop(0, ROWS, diagonal, 0)

    def pair(step):
        def run(n, carry):
            j = n * NBAND + 2 + step
            i = (n + step) * NBAND + 2 - step
            s = 0.5 * (w[j] * maskf[j] + (w[i] * maskf[i]).T)
            w[j] = s
            h, l = split(s)
            right_h[j], right_l[j] = h, l
            s = s.T
            w[i] = s
            h, l = split(s)
            right_h[i], right_l[i] = h, l
            return carry

        return run

    lax.fori_loop(0, ROWS - 1, pair(1), 0)
    lax.fori_loop(0, ROWS - 2, pair(2), 0)

    for side in range(2):
        first = w[DIAG[side][0]]
        packed[side] = jnp.where(rows > cols, first, w[DIAG[side][1]])
        d_out[side, 2:3, :] = jnp.sum(first * eye, axis=0, keepdims=True)

        @pl.when(exists(steps[side]))
        def _():
            for a in range(5):
                m_copy(side, a, 1 - side).start()

    right_h[BLOCKS] = jnp.zeros((B, B), BF16)
    right_l[BLOCKS] = jnp.zeros((B, B), BF16)
    for j in (0, 1, 8, 9):
        dinv[j] = jnp.ones((8, B), F32)

    for side in range(2):

        @pl.when(exists(steps[side]))
        def _():
            for a in range(3):
                w_copy(side, a, side, a).wait_recv()
            for a in range(3):
                w_copy(side, a, 1 - side, LANDS[a]).wait_send()

        for a in range(3):
            j = CROSS[side][a]
            s = 0.5 * (w[j] + w_in[side, a].T)
            w[j] = s
            h, l = split(s)
            right_h[j], right_l[j] = h, l

    def degrees(n, carry):
        a = w[n * NBAND]
        for t in range(1, NBAND):
            a = a + w[n * NBAND + t]
        a = a[:, :128] + a[:, 128:]
        dinv[n + 2] = jnp.broadcast_to(1.0 / jnp.sum(a.T, axis=0, keepdims=True), (8, B))
        return carry

    lax.fori_loop(0, ROWS, degrees, 0)

    for side in range(2):
        for a in range(2):
            d_out[side, a : a + 1, :] = dinv[2 + a if side == 0 else 7 - a, 0:1, :]
        d_out[side, 3:8, :] = jnp.zeros((5, B), F32)

        @pl.when(exists(steps[side]))
        def _():
            d_copy(side, 1 - side).start()

    def scale_left(j, carry):
        n, t = lax.div(j, NBAND), lax.rem(j, NBAND)
        h, l = split(w[j] * dinv[n + t, 0:1, :])
        left_h[j], left_l[j] = h, l
        return carry

    lax.fori_loop(0, BLOCKS, scale_left, 0)

    def local(i, carry):
        n = lax.div(i, CAPO)
        u = slots[i]
        total = None
        for t in range(NBAND):
            k, v = n + t - 2, u - t
            usable = (k >= 0) & (k < ROWS) & (u >= 0) & (v >= 0) & (v < NBAND)
            r = jnp.where(usable, k * NBAND + v, BLOCKS)
            j = n * NBAND + t
            term = product((left_h[j], left_l[j]), (right_h[r], right_l[r]))
            total = term if total is None else total + term
        inflated[i] = total
        return carry

    lax.fori_loop(0, SLOTS, local, 0)

    crossing = []
    for side in range(2):

        @pl.when(exists(steps[side]))
        def _():
            d_copy(side, side).wait_recv()

        for a in range(3):
            row = (0, 1, 0)[a]
            h, l = split(w[CROSS[side][a]] * d_in[side, row : row + 1, :])
            lx_h[side, a], lx_l[side, a] = h, l
        base = side * 12
        lefts = [(lx_h.at[side, a], lx_l.at[side, a]) for a in range(3)]
        owns = [(right_h.at[j], right_l.at[j]) for j in CROSS[side]]

        def mul(a, b, how, lefts=lefts):
            return product((lefts[a][0][...], lefts[a][1][...]), (b[0][...], b[1][...]), how)

        extra[base + 4] = mul(0, owns[0], dot_nt) + mul(1, owns[1], dot_nt)
        extra[base + 5] = mul(0, owns[2], dot_nt)
        extra[base + 10] = mul(2, owns[0], dot_nt)
        extra[base + 11] = mul(2, owns[2], dot_nt)
        extra[base + 6] = zero
        crossing.append((base, mul))

    def arrived(side, a):
        @pl.when(exists(steps[side]))
        def _():
            m_copy(side, a, side).wait_recv()

    for side in range(2):
        base, mul = crossing[side]
        arrived(side, 0)
        m = m_in[side, 0]
        mt = m.T
        near = jnp.where(rows > cols, m, mt)
        near = jnp.where(rows == cols, d_in[side, 2:3, :], near)
        h, l = split(near)
        m_h[side, 0], m_l[side, 0] = h, l
        h, l = split(jnp.where(rows > cols, mt, m))
        m_h[side, 5], m_l[side, 5] = h, l
        ref = lambda a, side=side: (m_h.at[side, a], m_l.at[side, a])
        extra[base + 9] = mul(2, ref(0), dot)
        for a in range(1, 5):
            arrived(side, a)
            h, l = split(m_in[side, a])
            m_h[side, a], m_l[side, a] = h, l
            if a == 1:
                extra[base + 3] = mul(0, ref(0), dot) + mul(1, ref(1), dot_nt)
                extra[base + 2] = mul(0, ref(1), dot) + mul(1, ref(5), dot)
                extra[base + 8] = mul(2, ref(1), dot)
            if a == 2:
                extra[base + 7] = mul(2, ref(2), dot)
            if a == 3:
                extra[base + 1] = mul(0, ref(2), dot) + mul(1, ref(3), dot)
            if a == 4:
                extra[base] = mul(1, ref(4), dot)

    def finish(i, carry):
        n = lax.div(i, CAPO)
        u = slots[i]
        low = n < 2
        inner = (n < 2) | (n >= ROWS - 2)
        near_row = jnp.where(low, n, ROWS - 1 - n)
        c = n + u - 4
        near_col = jnp.where(low, c, ROWS - 1 - c) + 4
        usable = inner & (u >= 0) & (near_col >= 0) & (near_col < 6)
        x = jnp.where(usable, jnp.where(low, 0, 12) + near_row * 6 + near_col, 6)
        y = inflated[i] + extra[x]
        y = y * y
        inflated[i] = y
        sums[pl.ds(i, 1), :] = jnp.sum(y, axis=0, keepdims=True)
        return carry

    lax.fori_loop(0, SLOTS, finish, 0)

    part[...] = jnp.dot(put[...], sums[...], precision=HIGHEST, preferred_element_type=F32)
    mirror = (1, 0, 3, 2)
    for j in range(4):

        @pl.when(exists(far[j]))
        def _():
            p_copy(j, mirror[j]).start()

    totals[...] = part[...]
    for j in range(4):

        @pl.when(exists(far[j]))
        def _():
            p_copy(j, j).wait_recv()

    totals[0:8, :] += part_in[0, 6:14, :]
    totals[6:14, :] += part_in[1, 0:8, :]
    totals[0:2, :] += part_in[2, 12:14, :]
    totals[12:14, :] += part_in[3, 0:2, :]
    chosen = pick[...]
    slot_totals = jnp.dot(chosen, totals[...], precision=HIGHEST, preferred_element_type=F32)
    live = jnp.sum(chosen, axis=1, keepdims=True) > 0.5
    scale[...] = jnp.where(live, B / jnp.where(live, slot_totals, 1.0), 0.0)

    for side in range(2):

        @pl.when(exists(steps[side]))
        def _():
            for a in range(5):
                m_copy(side, a, 1 - side).wait_send()
            d_copy(side, 1 - side).wait_send()

    for j in range(4):

        @pl.when(exists(far[j]))
        def _():
            p_copy(j, mirror[j]).wait_send()


def normalise(x, scale, out):
    for s in range(CAPO):
        out[s] = x[s] * scale[0, s : s + 1, :]


def body(names, sizes, weights, band_mask, out_slots):
    maskf = jnp.broadcast_to(band_mask.astype(F32).reshape(BLOCKS, 1, 1), (BLOCKS, 1, B))
    slots = out_slots.reshape(SLOTS)
    position = (jnp.arange(ROWS, dtype=jnp.int32)[:, None] + out_slots).reshape(SLOTS)
    columns = jnp.arange(COLS, dtype=jnp.int32)
    pick = ((position[:, None] == columns) & (slots[:, None] >= 0)).astype(F32)
    vmem = pl.BlockSpec(memory_space=pltpu.VMEM)
    dma = pltpu.SemaphoreType.DMA
    inflated, scale = pl.pallas_call(
        functools.partial(kernel, names, sizes),
        out_shape=(
            jax.ShapeDtypeStruct((SLOTS, B, B), F32),
            jax.ShapeDtypeStruct((SLOTS, B), F32),
        ),
        in_specs=[pl.BlockSpec(memory_space=pltpu.SMEM), pl.BlockSpec(memory_space=pl.ANY), vmem, vmem, vmem],
        out_specs=(vmem, vmem),
        scratch_shapes=[
            pltpu.VMEM((BLOCKS, B, B), F32),
            pltpu.VMEM((BLOCKS + 1, B, B), BF16),
            pltpu.VMEM((BLOCKS + 1, B, B), BF16),
            pltpu.VMEM((BLOCKS, B, B), BF16),
            pltpu.VMEM((BLOCKS, B, B), BF16),
            pltpu.VMEM((24, B, B), F32),
            pltpu.VMEM((2, B, B), F32),
            pltpu.VMEM((2, 3, B, B), F32),
            pltpu.VMEM((2, 5, B, B), F32),
            pltpu.VMEM((2, 6, B, B), BF16),
            pltpu.VMEM((2, 6, B, B), BF16),
            pltpu.VMEM((2, 3, B, B), BF16),
            pltpu.VMEM((2, 3, B, B), BF16),
            pltpu.VMEM((10, 8, B), F32),
            pltpu.VMEM((2, 8, B), F32),
            pltpu.VMEM((2, 8, B), F32),
            pltpu.VMEM((SLOTS, B), F32),
            pltpu.VMEM((COLS, B), F32),
            pltpu.VMEM((4, COLS, B), F32),
            pltpu.VMEM((COLS, B), F32),
            dma((7,)),
            dma((2, 3)),
            dma((2, 3)),
            dma((2, 5)),
            dma((2, 5)),
            dma((2,)),
            dma((2,)),
            dma((4,)),
            dma((4,)),
        ],
        compiler_params=pltpu.CompilerParams(
            collective_id=0, has_side_effects=True, vmem_limit_bytes=56 * 1024 * 1024
        ),
    )(slots, weights.reshape(BLOCKS, B, B), maskf, pick, pick.T)
    flow = pl.pallas_call(
        normalise,
        out_shape=jax.ShapeDtypeStruct((SLOTS, B, B), F32),
        grid=(ROWS,),
        in_specs=[
            pl.BlockSpec((CAPO, B, B), lambda i: (i, 0, 0)),
            pl.BlockSpec((1, CAPO, B), lambda i: (i, 0, 0)),
        ],
        out_specs=pl.BlockSpec((CAPO, B, B), lambda i: (i, 0, 0)),
    )(inflated, scale.reshape(ROWS, CAPO, B))
    return flow.reshape(ROWS, CAPO, B, B)


def solution(mesh):
    names = tuple(mesh.axis_names)
    sizes = tuple(mesh.shape[name] for name in names)
    return jax.shard_map(
        functools.partial(body, names, sizes),
        mesh=mesh,
        in_specs=(
            P(("row", "col"), None, None, None),
            P(("row", "col"), None),
            P(("row", "col"), None),
        ),
        out_specs=P(("row", "col"), None, None, None),
        check_vma=False,
    )
```

time: 358 us -> 84.2 us (0.24)
  local copies, waits for them, and re-layouts: 149 us -> 3.16 us
  starting transfers between devices: 80.6 us -> 0 us
  Pallas kernels: 0 us -> 78 us
  matrix products: 49.2 us -> 0 us
  other arithmetic: 46.3 us -> 2.66 us
  waiting for transfers between devices: 16.8 us -> 0 us
  loops' own time: 12.2 us -> 0 us
    gather x12 -> x0, local copies, waits for them, and re-layouts: 84.3 us -> none  [expand_local(): right_band[source_rows[None, :], picked]]
    ppermute x8 -> x0, starting transfers between devices: 80.6 us -> none  [the longest x3 72.7 us: with_halo(): lax.ppermute(tail, axis, [(i, (i + 1) % count) for i in range(ends)])]
    pallas_call x0 -> x2, Pallas kernels: none -> 78 us  [the longest x1 71.1 us: body(): pl.pallas_call(functools.partial(kernel, names, sizes), out_shape=(jax.Sh...]
    dot_general x8 -> x0, matrix products: 49.2 us -> none  [the longest x6 48.7 us: expand_local(): jnp.einsum('tij,stjk->sik', left_rows, right_rows, precision=highest)]
    unnamed x14 -> x3, local copies, waits for them, and re-layouts: 23.3 us -> 0.77 us
    slice x6 -> x0, local copies, waits for them, and re-layouts: 20 us -> none  [the longest x2 16.2 us: symmetrize(): own_rows = extended[W:W + row_count]]
    ppermute x8 -> x0, waiting for transfers between devices: 16.8 us -> none  [the longest x2 9.55 us: passed_along(): return lax.ppermute(value, axis, pairs)]
    concatenate x13 -> x0, other arithmetic: 13.6 us -> none  [the longest x1 9.05 us: with_halo(): jnp.concatenate([lax.ppermute(tail, axis, [(i, (i + 1) % count) for i in...]
  transfers between devices with their start and end apart: 8 -> 0, of which waited for: 4 -> 0; matrix products, arithmetic and copies ran while one was open for 4% -> 0% of each run, Pallas kernels for 0% -> 0%
where the time goes in v1:
time: 84.2 us; the launch traced here: 83.8 us
  Pallas kernels  78 us (93%)
  local copies, waits for them, and re-layouts  3.16 us (4%)
  other arithmetic  2.66 us (3%)
    pallas_call x1, Pallas kernels, body(): pl.pallas_call(functools.partial(kernel, names, sizes), out_shape=(jax.Sh...  71.1 us
    pallas_call x1, Pallas kernels, body(): pl.pallas_call(normalise, out_shape=jax.ShapeDtypeStruct((SLOTS, B, B), F...  6.85 us

profile of v1, /device:TPU:0, one launch (start us, length us, event | category | flops | bytes accessed | tf_op | source)
XLA Modules:
  0.0 83.8 jit_solution(12218846778619002737)
XLA Ops:
  0.0 0.7 iota_add_fusion
  0.7 0.1 copy.7
  0.8 0.1 eq.22
  0.9 0.7 convert_element_type.8
  1.6 0.1 broadcast_in_dim.4
  1.6 0.8 copy.6
  2.4 0.1 reshape.24.slots
  2.5 0.0 copy-start
  2.5 0.6 fusion.3.put
  3.1 0.7 fusion.1.pick
  3.8 0.7 broadcast_in_dim.10.maskf
  4.5 0.0 copy-done
  4.5 71.1 %shard_map.37 = (f32[24,256,256]{2,1,0:T(8,128)}, f32[24,256]{1,0:T(8,128)}) custom-call(s32[24]{0:T(128)} %copy-done, f32[30,256,256]{2,1,0:T(8,128)} %bitcast.2, f32[30,1,256]{2,1,0:T(1,128)} %broadcast_in_dim.10.maskf, f32[24,16]{1,0:T(8,128)} %fusion.1.pick, f32[16,24]{1,0:T(8,128)} %fusion.3.put), custom_call_target="tpu_custom_call" | custom-call | tf_op jit(solution)/shard_map/pallas_call | solution.py:371
  75.6 1.3 %reshape.26.scale = f32[6,4,256]{2,1,0:T(4,128)} reshape(f32[24,256]{1,0:T(8,128)} %get-tuple-element.8) | data formatting | bytes 49152 | tf_op jit(solution)/shard_map/reshape | solution.py:423
  76.9 6.9 %shard_map.38 = f32[24,256,256]{2,1,0:T(8,128)} custom-call(f32[24,256,256]{2,1,0:T(8,128)} %get-tuple-element.7.x, f32[6,4,256]{2,1,0:T(4,128)} %reshape.26.scale), custom_call_target="tpu_custom_call" | custom-call | tf_op jit(solution)/shard_map/pallas_call | solution.py:414
  (1 shorter events, 0.0 us)
Async XLA Ops:
  2.5 2.0 %copy-start = (s32[24]{0:T(128)}, s32[24]{0:T(128)S(1)}, u32[]{:S(2)}) copy-start(s32[24]{0:T(128)S(1)} %reshape.24.slots) | copy-start | bytes 292

commit v2 on v1

--- a/solution.py
+++ b/solution.py
@@ -20,7 +20,6 @@
 LANDS = (0, 2, 1)
 INNER = ((3, 4, 8, 9), (26, 25, 21, 20))
 DIAG = ((2, 7), (27, 22))
-HIGHEST = lax.Precision.HIGHEST
 
 
 def split(x):
@@ -42,10 +41,10 @@
 
 def kernel(
     names, sizes,
-    slots, w_hbm, maskf, pick, put,
+    slots, mask, w_hbm,
     inflated, scale,
     w, right_h, right_l, left_h, left_l, extra, packed, w_in, m_in, m_h, m_l, lx_h, lx_l,
-    dinv, d_out, d_in, sums, part, part_in, totals,
+    dinv, d_out, d_in, part, part_in, totals,
     load_sem, w_send, w_recv, m_send, m_recv, d_send, d_recv, p_send, p_recv,
 ):
     ncol = sizes[1]
@@ -79,7 +78,7 @@
     for copy in loads[:4]:
         copy.wait()
     for j in (0, 1, 5, 24, 28, 29):
-        w[j] = w[j] * maskf[j]
+        w[j] = w[j] * mask[j // NBAND, j % NBAND].astype(F32)
 
     peers = sum(exists(by).astype(jnp.int32) for by in far)
     pl.semaphore_wait(barrier, peers)
@@ -138,7 +137,7 @@
 
     def diagonal(n, carry):
         j = n * NBAND + 2
-        x = w[j] * maskf[j]
+        x = w[j] * mask[n, 2].astype(F32)
         s = 0.5 * (x + x.T) + eye
         w[j] = s
         h, l = split(s)
@@ -151,7 +150,8 @@
         def run(n, carry):
             j = n * NBAND + 2 + step
             i = (n + step) * NBAND + 2 - step
-            s = 0.5 * (w[j] * maskf[j] + (w[i] * maskf[i]).T)
+            upper = w[j] * mask[n, 2 + step].astype(F32)
+            s = 0.5 * (upper + (w[i] * mask[n + step, 2 - step].astype(F32)).T)
             w[j] = s
             h, l = split(s)
             right_h[j], right_l[j] = h, l
@@ -224,21 +224,40 @@
 
     lax.fori_loop(0, BLOCKS, scale_left, 0)
 
-    def local(i, carry):
-        n = lax.div(i, CAPO)
-        u = slots[i]
-        total = None
-        for t in range(NBAND):
-            k, v = n + t - 2, u - t
-            usable = (k >= 0) & (k < ROWS) & (u >= 0) & (v >= 0) & (v < NBAND)
-            r = jnp.where(usable, k * NBAND + v, BLOCKS)
-            j = n * NBAND + t
-            term = product((left_h[j], left_l[j]), (right_h[r], right_l[r]))
-            total = term if total is None else total + term
+    def term(n, t, u, live):
+        v = u - t
+        r = jnp.where(live & (v >= 0) & (v < NBAND), (n + t - 2) * NBAND + v, BLOCKS)
+        j = n * NBAND + t
+        return product((left_h[j], left_l[j]), (right_h[r], right_l[r]))
+
+    def end_rows(i, carry):
+        n = jnp.where(i < CAPO, 0, ROWS - 1)
+        s = lax.rem(i, CAPO)
+        u = slots[n, s]
+        first = jnp.where(i < CAPO, 2, 0)
+        total = term(n, first, u, u >= 0)
+        for t in range(1, 3):
+            total = total + term(n, first + t, u, u >= 0)
+        inflated[n * CAPO + s] = total
+        return carry
+
+    def middle_rows(i, carry):
+        n, s = lax.div(i, CAPO), lax.rem(i, CAPO)
+        u = slots[n, s]
+        first = jnp.where(n == 1, 1, jnp.where(n == 4, 0, (u > 4).astype(jnp.int32)))
+        total = term(n, first, u, u >= 0)
+        for t in range(1, 4):
+            total = total + term(n, first + t, u, u >= 0)
         inflated[i] = total
         return carry
 
-    lax.fori_loop(0, SLOTS, local, 0)
+    def last_terms(n, carry):
+        inflated[n * CAPO] += term(n, 4, 4, True)
+        return carry
+
+    lax.fori_loop(0, 2 * CAPO, end_rows, 0)
+    lax.fori_loop(CAPO, SLOTS - CAPO, middle_rows, 0)
+    lax.fori_loop(2, 4, last_terms, 0)
 
     crossing = []
     for side in range(2):
@@ -298,9 +317,12 @@
             if a == 4:
                 extra[base] = mul(1, ref(4), dot)
 
+    lines = lax.broadcasted_iota(jnp.int32, (COLS, B), 0)
+    part[...] = jnp.zeros((COLS, B), F32)
+
     def finish(i, carry):
         n = lax.div(i, CAPO)
-        u = slots[i]
+        u = slots[n, lax.rem(i, CAPO)]
         low = n < 2
         inner = (n < 2) | (n >= ROWS - 2)
         near_row = jnp.where(low, n, ROWS - 1 - n)
@@ -311,12 +333,12 @@
         y = inflated[i] + extra[x]
         y = y * y
         inflated[i] = y
-        sums[pl.ds(i, 1), :] = jnp.sum(y, axis=0, keepdims=True)
+        here = (lines == n + u) & (u >= 0)
+        part[...] += jnp.where(here, jnp.sum(y, axis=0, keepdims=True), 0.0)
         return carry
 
     lax.fori_loop(0, SLOTS, finish, 0)
 
-    part[...] = jnp.dot(put[...], sums[...], precision=HIGHEST, preferred_element_type=F32)
     mirror = (1, 0, 3, 2)
     for j in range(4):
 
@@ -335,10 +357,12 @@
     totals[6:14, :] += part_in[1, 0:8, :]
     totals[0:2, :] += part_in[2, 12:14, :]
     totals[12:14, :] += part_in[3, 0:2, :]
-    chosen = pick[...]
-    slot_totals = jnp.dot(chosen, totals[...], precision=HIGHEST, preferred_element_type=F32)
-    live = jnp.sum(chosen, axis=1, keepdims=True) > 0.5
-    scale[...] = jnp.where(live, B / jnp.where(live, slot_totals, 1.0), 0.0)
+    everything = totals[...]
+
+    for i in range(SLOTS):
+        u = slots[i // CAPO, i % CAPO]
+        mine = jnp.sum(jnp.where(lines == i // CAPO + u, everything, 0.0), axis=0, keepdims=True)
+        scale[i : i + 1, :] = jnp.where(u >= 0, B / jnp.where(u >= 0, mine, 1.0), 0.0)
 
     for side in range(2):
 
@@ -355,26 +379,33 @@
             p_copy(j, mirror[j]).wait_send()
 
 
-def normalise(x, scale, out):
-    for s in range(CAPO):
-        out[s] = x[s] * scale[0, s : s + 1, :]
+def normalise(x, scale, flow, out, sems):
+    copies = []
+    for n in range(ROWS):
+        for j in range(n * CAPO, (n + 1) * CAPO):
+            out[j] = x[j] * scale[j : j + 1, :]
+        rows = pl.ds(n * CAPO, CAPO)
+        copy = pltpu.make_async_copy(out.at[rows], flow.at[rows], sems.at[n])
+        copy.start()
+        copies.append(copy)
+    for copy in copies:
+        copy.wait()
 
 
 def body(names, sizes, weights, band_mask, out_slots):
-    maskf = jnp.broadcast_to(band_mask.astype(F32).reshape(BLOCKS, 1, 1), (BLOCKS, 1, B))
-    slots = out_slots.reshape(SLOTS)
-    position = (jnp.arange(ROWS, dtype=jnp.int32)[:, None] + out_slots).reshape(SLOTS)
-    columns = jnp.arange(COLS, dtype=jnp.int32)
-    pick = ((position[:, None] == columns) & (slots[:, None] >= 0)).astype(F32)
     vmem = pl.BlockSpec(memory_space=pltpu.VMEM)
     dma = pltpu.SemaphoreType.DMA
     inflated, scale = pl.pallas_call(
         functools.partial(kernel, names, sizes),
         out_shape=(
-            jax.ShapeDtypeStruct((SLOTS, B, B), F32),
-            jax.ShapeDtypeStruct((SLOTS, B), F32),
+            pltpu.VMEM((SLOTS, B, B), F32),
+            pltpu.VMEM((SLOTS, B), F32),
         ),
-        in_specs=[pl.BlockSpec(memory_space=pltpu.SMEM), pl.BlockSpec(memory_space=pl.ANY), vmem, vmem, vmem],
+        in_specs=[
+            pl.BlockSpec(memory_space=pltpu.SMEM),
+            pl.BlockSpec(memory_space=pltpu.SMEM),
+            pl.BlockSpec(memory_space=pl.ANY),
+        ],
         out_specs=(vmem, vmem),
         scratch_shapes=[
             pltpu.VMEM((BLOCKS, B, B), F32),
@@ -393,7 +424,6 @@
             pltpu.VMEM((10, 8, B), F32),
             pltpu.VMEM((2, 8, B), F32),
             pltpu.VMEM((2, 8, B), F32),
-            pltpu.VMEM((SLOTS, B), F32),
             pltpu.VMEM((COLS, B), F32),
             pltpu.VMEM((4, COLS, B), F32),
             pltpu.VMEM((COLS, B), F32),
@@ -408,19 +438,17 @@
             dma((4,)),
         ],
         compiler_params=pltpu.CompilerParams(
-            collective_id=0, has_side_effects=True, vmem_limit_bytes=56 * 1024 * 1024
+            collective_id=0, has_side_effects=True, vmem_limit_bytes=46 * 1024 * 1024
         ),
-    )(slots, weights.reshape(BLOCKS, B, B), maskf, pick, pick.T)
+    )(out_slots, band_mask, weights.reshape(BLOCKS, B, B))
     flow = pl.pallas_call(
         normalise,
         out_shape=jax.ShapeDtypeStruct((SLOTS, B, B), F32),
-        grid=(ROWS,),
-        in_specs=[
-            pl.BlockSpec((CAPO, B, B), lambda i: (i, 0, 0)),
-            pl.BlockSpec((1, CAPO, B), lambda i: (i, 0, 0)),
-        ],
-        out_specs=pl.BlockSpec((CAPO, B, B), lambda i: (i, 0, 0)),
-    )(inflated, scale.reshape(ROWS, CAPO, B))
+        in_specs=[vmem, vmem],
+        out_specs=pl.BlockSpec(memory_space=pl.ANY),
+        scratch_shapes=[pltpu.VMEM((SLOTS, B, B), F32), dma((ROWS,))],
+        compiler_params=pltpu.CompilerParams(vmem_limit_bytes=20 * 1024 * 1024),
+    )(inflated, scale)
     return flow.reshape(ROWS, CAPO, B, B)
 
 

time: 84.2 us -> 69.6 us (0.83)
  Pallas kernels: 78 us -> 67.9 us
  other arithmetic: 2.66 us -> 0 us
  local copies, waits for them, and re-layouts: 3.16 us -> 1.45 us
    pallas_call x1, Pallas kernels: 71.1 us -> 65.1 us  [body(): pl.pallas_call(functools.partial(kernel, names, sizes), out_shape=(pltpu....]
    pallas_call x1, Pallas kernels: 6.85 us -> 2.79 us  [body(): pl.pallas_call(normalise, out_shape=jax.ShapeDtypeStruct((SLOTS, B, B), F...]
    convert_element_type x3 -> x0, other arithmetic: 1.97 us -> none  [the longest x2 1.27 us: body(): pick = ((position[:, None] == columns) & (slots[:, None] >= 0)).astype(F32)]
    reshape x2 -> x0, local copies, waits for them, and re-layouts: 1.43 us -> none  [the longest x1 1.35 us: body(): scale.reshape(ROWS, CAPO, B)]
where the time goes in v2:
time: 69.6 us; the launch traced here: 69.4 us
  Pallas kernels  67.9 us (98%)
  local copies, waits for them, and re-layouts  1.45 us (2%)
    pallas_call x1, Pallas kernels, body(): pl.pallas_call(functools.partial(kernel, names, sizes), out_shape=(pltpu....  65.1 us
    pallas_call x1, Pallas kernels, body(): pl.pallas_call(normalise, out_shape=jax.ShapeDtypeStruct((SLOTS, B, B), F...  2.79 us
    unnamed x3, local copies, waits for them, and re-layouts  1.45 us

profile of v2, /device:TPU:0, one launch (start us, length us, event | category | flops | bytes accessed | tf_op | source)
XLA Modules:
  0.0 69.4 jit_solution(7833533829868459379)
XLA Ops:
  0.0 0.8 %copy.4.slots = s32[6,4]{1,0:T(8,128)S(1)} copy(s32[6,4]{0,1:T(4,128)} %param.5) | data formatting | bytes 192 | tf_op args[2]
  0.8 0.0 copy-start
  0.8 0.7 copy-done
  1.5 65.1 %shard_map.37 = (f32[24,256,256]{2,1,0:T(8,128)S(1)}, f32[24,256]{1,0:T(8,128)S(1)}) custom-call(s32[6,4]{1,0:T(8,128)S(1)} %copy.4.slots, s32[6,5]{1,0:T(8,128)S(1)} %copy-done, f32[30,256,256]{2,1,0:T(8,128)} %bitcast.2), custom_call_target="tpu_custom_call" | custom-call | tf_op jit(solution)/shard_map/pallas_call | solution.py:398
  66.6 2.8 %shard_map.38 = f32[24,256,256]{2,1,0:T(8,128)} custom-call(f32[24,256,256]{2,1,0:T(8,128)S(1)} %get-tuple-element.7.x, f32[24,256]{1,0:T(8,128)S(1)} %get-tuple-element.8.scale), custom_call_target="tpu_custom_call" | custom-call | tf_op jit(solution)/shard_map/pallas_call | solution.py:444
Async XLA Ops:
  0.8 0.7 copy-start
